TPU v7x, 256 devices: a whole 4x4x8 slice. The times are simulated.
256 devices in a mesh: sample: 8 (over y, z_hi), slab: 32 (over z_lo, x, core).
Axes of the slice: x: 4, y: 4, z: 8 (z_hi: 2, z_lo: 4; z = z_hi * 4 + z_lo), core: 2. Of those that a mesh axis runs over, the one named last changes fastest.
Arguments:
- volume: bfloat16 [8, 64, 32, 2048], P('sample', 'slab'), may hold values from -6 to 6
- cotangent: bfloat16 [8, 64, 32, 2048], P('sample', 'slab'), may hold values from -6 to 6
- first_weight: bfloat16 [3, 3, 3, 64, 64], replicated, may hold values from -0.15625 to 0.15625
- second_weight: bfloat16 [3, 3, 3, 64, 64], replicated, may hold values from -0.15625 to 0.15625
Outputs:
- features_out: bfloat16 [8, 64, 32, 2048], P('sample', 'slab')
- input_grad: bfloat16 [8, 64, 32, 2048], P('sample', 'slab')
- first_grad: float32 [110592], P(('sample', 'slab'))
- second_grad: float32 [110592], P(('sample', 'slab'))
All inputs are finite; a program needn't handle non-finite values.
Results may differ from a plain program's by a relative error of at most 0.024.
Values may be sent and summed in bfloat16 or wider, within the bound.
A program may use at most 64 MiB of HBM per device.

v0:
```python
import functools
import math

import jax
import jax.numpy as jnp
from jax import lax
from jax.experimental import pallas as pl
from jax.experimental.pallas import tpu as pltpu
from jax.sharding import PartitionSpec as P

MESH = pl.DeviceIdType.MESH
BF16 = jnp.bfloat16
F32 = jnp.float32

C = 64
CELLS = 32
MERGED = 2048
QUADS = 8
WINDOW = 384
WIDE = 3 * WINDOW
TAPROWS = 864
OFFSETS = (0, 1, 2, 3, 4, -1)


def dot(a, b):
    return lax.dot_general(a, b, (((1,), (0,)), ((), ())), preferred_element_type=F32)


def sigmoid(v):
    return 0.5 * jnp.tanh(0.5 * v) + 0.5


def prepare(src, plane, win, slot):
    rows = lax.broadcasted_iota(jnp.int32, (CELLS, 128), 0)
    low_half = lax.broadcasted_iota(jnp.int32, (CELLS, 128), 1) < C
    base = slot * 256

    def shifted(tile):
        here = src[plane, :, tile * 128 : tile * 128 + 128].astype(F32)
        before = jnp.where(rows == 0, 0.0, pltpu.roll(here, 1, 0))
        after = jnp.where(rows == CELLS - 1, 0.0, pltpu.roll(here, CELLS - 1, 0))
        return before.astype(BF16), here.astype(BF16), after.astype(BF16)

    nothing = jnp.zeros((CELLS, 128), BF16)
    blank = (nothing, nothing, nothing)
    tiles = {-1: blank, 16: blank}
    for tile in range(16):
        tiles[tile] = shifted(tile)
    for j in range(QUADS):
        at = pl.ds(pl.multiple_of(base + j * CELLS, CELLS), CELLS)
        for d in range(3):
            edge = jnp.where(low_half, tiles[2 * j + 2][d], tiles[2 * j - 1][d])
            win[at, d * WINDOW : d * WINDOW + 128] = tiles[2 * j][d]
            win[at, d * WINDOW + 128 : d * WINDOW + 256] = tiles[2 * j + 1][d]
            win[at, d * WINDOW + 256 : d * WINDOW + 384] = edge


def transpose_plane(win, slot, out, to):
    rows = pl.ds(pl.multiple_of(slot * 256, 256), 256)
    out[pl.ds(pl.multiple_of(to * 256, 256), 256), :] = win[rows, WINDOW : WINDOW + 256].T


def expand_weight(weight, forward, backward):
    zero = jnp.zeros((C, C), BF16)
    blank = jnp.zeros((C, 128), BF16)

    def tap(index, carry):
        kx = index // 3
        ky = index % 3
        m = [weight[kx, ky, kz] for kz in range(3)]
        pair = jnp.concatenate([m[0], m[1]], axis=1).astype(F32).T.astype(BF16)
        last = jnp.concatenate([m[2], zero], axis=1).astype(F32).T.astype(BF16)
        n = [pair[:C], pair[C:], last[:C]]
        cat = lambda a, b: jnp.concatenate([a, b], axis=1)
        ahead = (cat(m[0], zero), cat(m[1], m[0]), cat(m[2], m[1]), cat(zero, m[2]))
        back = (cat(zero, n[0]), cat(n[0], n[1]), cat(n[1], n[2]), cat(n[2], zero))
        for w, offset in enumerate(OFFSETS):
            there = pl.ds(pl.multiple_of(ky * WINDOW + w * C, C), C)
            mirrored = pl.ds(pl.multiple_of((2 - ky) * WINDOW + w * C, C), C)
            for half in range(2):
                a = offset - 2 * half + 1
                b = 2 * half - offset + 2
                cols = slice(128 * half, 128 * half + 128)
                forward[kx, there, cols] = ahead[a] if 0 <= a < 4 else blank
                backward[2 - kx, mirrored, cols] = back[b] if 0 <= b < 4 else blank
        return carry

    lax.fori_loop(0, 9, tap, 0)


def convolve(win, first, planes, weight):
    total = None
    for e in range(3):
        lhs = win[(first + e) * 256 : (first + e + planes) * 256, :]
        term = dot(lhs, weight[e])
        total = term if total is None else total + term
    return total


def kernel_gradient(flipped, win, first, product, flat):
    whole = dot(flipped[0:768], win[first * 256 : first * 256 + 256, :]) + dot(
        flipped[256:1024], win[first * 256 + 256 : first * 256 + 512, :]
    )
    for tile in range(9):
        product[tile] = whole[:, tile * 128 : tile * 128 + 128]
    low_half = lax.broadcasted_iota(jnp.int32, (32, 128), 1) < C

    for e in range(3):
        for ky in range(3):
            column = (2 - ky) * 3

            def part(zi, tile, parity):
                return product[column + tile, pl.ds(e * 256 + zi * C + parity, 32, stride=2), :]

            sums = {}
            for parity in range(2):
                sums[0, parity] = (
                    part(1, 1, parity) + part(3, 2, parity),
                    part(0, 0, parity) + part(2, 1, parity),
                )
                sums[1, parity] = (
                    part(0, 0, parity) + part(2, 1, parity),
                    part(1, 0, parity) + part(3, 1, parity),
                )
                sums[2, parity] = (
                    part(1, 0, parity) + part(3, 1, parity),
                    part(0, 2, parity) + part(2, 0, parity),
                )
            for kz in range(3):
                low0, high0 = sums[kz, 0]
                low1, high1 = sums[kz, 1]
                straight = jnp.where(low_half, low0, high1)
                crossed = jnp.where(low_half, low1, high0)
                tap = (e * 3 + ky) * 3 + kz
                flat[tap * 32 : tap * 32 + 32, :] = straight + pltpu.roll(crossed, C, 1)


def kernel(
    vol_hbm,
    cot_hbm,
    w1_hbm,
    w2_hbm,
    feat_hbm,
    back_hbm,
    first_out,
    second_out,
    vol,
    cot,
    w1,
    w2,
    ahead1,
    back1,
    ahead2,
    back2,
    win_v,
    win_h,
    win_g2,
    win_g1,
    flipped,
    hid,
    g2,
    g1,
    feat,
    back,
    pre,
    own_pre,
    acc,
    product,
    flat,
    near,
    near_in,
    far,
    far_in,
    load_sem,
    store_sem,
    vol_send,
    vol_recv,
    g_send,
    g_recv,
    near_send,
    near_recv,
    far_send,
    far_recv,
    *,
    slabs,
    scale,
):
    sample = lax.axis_index("sample")
    slab = lax.axis_index("slab")
    y, z_hi = sample // 2, sample % 2
    z_lo, x, core = slab // 8, (slab % 8) // 2, slab % 2
    z = z_hi * 4 + z_lo

    def near_partner(r):
        return (((y + r // 4) % 4) * 2 + z_hi, z_lo * 8 + ((x + r % 4) % 4) * 2 + core)

    def far_partner(r):
        zz = (z + r // 2) % 8
        return (y * 2 + zz // 4, (zz % 4) * 8 + x * 2 + (core + r % 2) % 2)

    has_low = slab > 0
    has_high = slab < slabs - 1
    low = (sample, slab - 1)
    high = (sample, slab + 1)

    barrier = pltpu.get_barrier_semaphore()

    @pl.when(has_low)
    def _():
        pl.semaphore_signal(barrier, inc=1, device_id=low, device_id_type=MESH)

    @pl.when(has_high)
    def _():
        pl.semaphore_signal(barrier, inc=1, device_id=high, device_id_type=MESH)

    def greet(r, carry):
        pl.semaphore_signal(barrier, inc=1, device_id=near_partner(r), device_id_type=MESH)
        pl.semaphore_signal(barrier, inc=1, device_id=far_partner(r), device_id_type=MESH)
        return carry

    lax.fori_loop(1, 16, greet, 0)

    loads = [
        pltpu.make_async_copy(w1_hbm, w1, load_sem.at[0]),
        pltpu.make_async_copy(vol_hbm.at[0], vol.at[2:4], load_sem.at[1]),
        pltpu.make_async_copy(w2_hbm, w2, load_sem.at[2]),
        pltpu.make_async_copy(cot_hbm.at[0], cot, load_sem.at[3]),
    ]
    for load in loads:
        load.start()

    neighbours = has_low.astype(jnp.int32) + has_high.astype(jnp.int32)
    pl.semaphore_wait(barrier, 30 + neighbours)

    def to_low(plane):
        return pltpu.make_async_remote_copy(
            vol_hbm.at[0, plane], vol.at[4 + plane], vol_send.at[plane], vol_recv.at[2 + plane], low, MESH
        )

    def to_high(plane):
        return pltpu.make_async_remote_copy(
            vol_hbm.at[0, plane], vol.at[plane], vol_send.at[2 + plane], vol_recv.at[plane], high, MESH
        )

    @pl.when(has_low)
    def _():
        to_low(0).start()

    @pl.when(has_high)
    def _():
        to_high(1).start()

    @pl.when(has_low)
    def _():
        to_low(1).start()

    @pl.when(has_high)
    def _():
        to_high(0).start()

    no_plane = jnp.zeros((CELLS, MERGED), BF16)

    @pl.when(jnp.logical_not(has_low))
    def _():
        for buffer, slots in ((vol, (0, 1)), (g2, (0,)), (g1, (0,))):
            for slot in slots:
                buffer[slot] = no_plane

    @pl.when(jnp.logical_not(has_high))
    def _():
        for buffer, slots in ((vol, (4, 5)), (g2, (3,)), (g1, (3,))):
            for slot in slots:
                buffer[slot] = no_plane

    flat[TAPROWS : TAPROWS + 8, :] = jnp.zeros((8, 128), F32)
    loads[0].wait()
    expand_weight(w1, ahead1, back1)
    loads[1].wait()
    prepare(vol, 2, win_v, 2)
    prepare(vol, 3, win_v, 3)
    loads[2].wait()
    expand_weight(w2, ahead2, back2)

    @pl.when(has_low)
    def _():
        to_high(1).wait_recv()

    @pl.when(has_high)
    def _():
        to_low(0).wait_recv()

    def prepare_pair(src, win, slots):
        def body(i, carry):
            slot = slots[0] + i * (slots[1] - slots[0])
            prepare(src, slot, win, slot)
            return carry

        lax.fori_loop(0, 2, body, 0)

    prepare_pair(vol, win_v, (1, 4))
    own_pre[...] = convolve(win_v, 1, 2, ahead1)

    @pl.when(has_low)
    def _():
        to_high(0).wait_recv()

    @pl.when(has_high)
    def _():
        to_low(1).wait_recv()

    prepare_pair(vol, win_v, (0, 5))
    pre[0:256, :] = convolve(win_v, 0, 1, ahead1)
    pre[256:512, :] = convolve(win_v, 3, 1, ahead1)

    def hide(source, at, plane, keep):
        for j in range(QUADS):
            value = source[pl.ds(pl.multiple_of(at + j * CELLS, CELLS), CELLS), :]
            value = value * sigmoid(value)
            if keep is not None:
                value = jnp.where(keep, value, 0.0)
            hid[plane, :, j * 256 : j * 256 + 256] = value.astype(BF16)

    hide(pre, 0, 0, has_low)
    hide(own_pre, 0, 1, None)
    hide(own_pre, 256, 2, None)
    hide(pre, 256, 3, has_high)
    prepare_pair(hid, win_h, (0, 1))
    prepare_pair(hid, win_h, (2, 3))
    acc[...] = convolve(win_h, 0, 2, ahead2)

    loads[3].wait()

    def second_stage(plane, carry):
        for j in range(QUADS):
            value = acc[pl.ds(pl.multiple_of(plane * 256 + j * CELLS, CELLS), CELLS), :]
            gate = sigmoid(value)
            cols = slice(j * 256, j * 256 + 256)
            feat[plane, :, cols] = (value * gate).astype(BF16)
            slope = gate * (1.0 + value * (1.0 - gate))
            g2[plane + 1, :, cols] = (cot[plane, :, cols].astype(F32) * slope).astype(BF16)
        return carry

    lax.fori_loop(0, 2, second_stage, 0)

    def halo(buffer, which, side):
        if side == 0:
            return pltpu.make_async_remote_copy(
                buffer.at[1], buffer.at[3], g_send.at[2 * which], g_recv.at[2 * which], low, MESH
            )
        return pltpu.make_async_remote_copy(
            buffer.at[2], buffer.at[0], g_send.at[2 * which + 1], g_recv.at[2 * which + 1], high, MESH
        )

    def send_halos(buffer, which):
        @pl.when(has_low)
        def _():
            halo(buffer, which, 0).start()

        @pl.when(has_high)
        def _():
            halo(buffer, which, 1).start()

    def receive_halos(buffer, which):
        @pl.when(has_high)
        def _():
            halo(buffer, which, 0).wait_recv()

        @pl.when(has_low)
        def _():
            halo(buffer, which, 1).wait_recv()

    send_halos(g2, 0)
    features_store = pltpu.make_async_copy(feat, feat_hbm.at[0], store_sem.at[0])
    features_store.start()

    me_near = y * 4 + x

    def near_copy(which, r):
        other = ((y + r // 4) % 4) * 4 + (x + r % 4) % 4
        return pltpu.make_async_remote_copy(
            near.at[which, other],
            near_in.at[which, r],
            near_send.at[which, r],
            near_recv.at[which, r],
            near_partner(r),
            MESH,
        )

    def far_copy(which, r):
        zz = (z + r // 2) % 8
        return pltpu.make_async_remote_copy(
            far.at[which, zz], far_in.at[which, r], far_send.at[which, r], far_recv.at[which, r], far_partner(r), MESH
        )

    def each(copy, what, which):
        def body(r, carry):
            getattr(copy(which, r), what)()
            return carry

        lax.fori_loop(1, 16, body, 0)

    def send_near(which):
        def row(yy, carry):
            for xx in range(4):
                for pair in range(4):
                    starts = [yy * 216 + (2 * pair + i) * 27 + (27 * xx) // 4 for i in range(2)]
                    both = jnp.concatenate([flat[pl.ds(s, 8), :] for s in starts], axis=0)
                    near[which, yy * 4 + xx, 16 * pair : 16 * pair + 16, :] = both.astype(BF16)
            return carry

        lax.fori_loop(0, 4, row, 0)
        each(near_copy, "start", which)

    def send_far(which):
        each(near_copy, "wait_recv", which)
        total = near[which, me_near].astype(F32)
        for r in range(1, 16):
            total = total + near_in[which, r].astype(F32)
        for zz in range(8):
            far[which, zz] = total[8 * zz : 8 * zz + 8]
        each(far_copy, "start", which)

    lane = lax.broadcasted_iota(jnp.int32, (8, 128), 1)
    begin = (96 * x) % 128 + 432 * core
    skip_rows, skip_lanes = begin // 128, begin % 128

    def finish(which, out):
        each(far_copy, "wait_recv", which)
        total = far[which, z]
        for r in range(1, 16):
            total = total + far_in[which, r]
        total = pltpu.roll(total * scale, (128 - skip_lanes) % 128, 1)
        upper = pltpu.roll(total, (8 - skip_rows) % 8, 0)
        lower = pltpu.roll(total, (8 - skip_rows + 7) % 8, 0)
        out[...] = jnp.where(lane < 128 - skip_lanes, upper, lower)

    prepare_pair(g2, win_g2, (1, 2))

    def flip_planes(win, first):
        def body(i, carry):
            transpose_plane(win, first + i, flipped, i)
            return carry

        lax.fori_loop(0, 4, body, 0)

    flip_planes(win_h, 0)
    kernel_gradient(flipped, win_g2, 1, product, flat)
    send_near(1)

    receive_halos(g2, 0)
    prepare_pair(g2, win_g2, (0, 3))
    acc[...] = convolve(win_g2, 0, 2, back2)

    def first_stage(plane, carry):
        for j in range(QUADS):
            at = pl.ds(pl.multiple_of(plane * 256 + j * CELLS, CELLS), CELLS)
            value = own_pre[at, :]
            gate = sigmoid(value)
            slope = gate * (1.0 + value * (1.0 - gate))
            g1[plane + 1, :, j * 256 : j * 256 + 256] = (acc[at, :] * slope).astype(BF16)
        return carry

    lax.fori_loop(0, 2, first_stage, 0)
    send_halos(g1, 1)

    prepare_pair(g1, win_g1, (1, 2))
    flip_planes(win_v, 1)
    kernel_gradient(flipped, win_g1, 1, product, flat)
    send_near(0)
    send_far(1)

    receive_halos(g1, 1)
    prepare_pair(g1, win_g1, (0, 3))
    acc[...] = convolve(win_g1, 0, 2, back1)
    for plane in range(2):
        for j in range(QUADS):
            at = (plane * QUADS + j) * CELLS
            back[plane, :, j * 256 : j * 256 + 256] = acc[at : at + CELLS, :].astype(BF16)
    back_store = pltpu.make_async_copy(back, back_hbm.at[0], store_sem.at[1])
    back_store.start()

    send_far(0)
    finish(1, second_out)
    finish(0, first_out)

    @pl.when(has_low)
    def _():
        to_low(0).wait_send()
        to_low(1).wait_send()
        halo(g2, 0, 0).wait_send()
        halo(g1, 1, 0).wait_send()

    @pl.when(has_high)
    def _():
        to_high(0).wait_send()
        to_high(1).wait_send()
        halo(g2, 0, 1).wait_send()
        halo(g1, 1, 1).wait_send()

    for which in range(2):
        each(near_copy, "wait_send", which)
        each(far_copy, "wait_send", which)
    features_store.wait()
    back_store.wait()


def per_device(volume, cotangent, first_weight, second_weight, *, slabs, voxels):
    vmem = lambda shape, dtype=BF16: pltpu.VMEM(shape, dtype)
    scratch = [
        vmem((6, CELLS, MERGED)),
        vmem((2, CELLS, MERGED)),
        vmem((3, 3, 3, C, C)),
        vmem((3, 3, 3, C, C)),
        vmem((3, WIDE, 256)),
        vmem((3, WIDE, 256)),
        vmem((3, WIDE, 256)),
        vmem((3, WIDE, 256)),
        vmem((6 * 256, WIDE)),
        vmem((4 * 256, WIDE)),
        vmem((4 * 256, WIDE)),
        vmem((4 * 256, WIDE)),
        vmem((1024, 256)),
        vmem((4, CELLS, MERGED)),
        vmem((4, CELLS, MERGED)),
        vmem((4, CELLS, MERGED)),
        vmem((2, CELLS, MERGED)),
        vmem((2, CELLS, MERGED)),
        vmem((512, 256), F32),
        vmem((512, 256), F32),
        vmem((512, 256), F32),
        vmem((9, 768, 128), F32),
        vmem((TAPROWS + 8, 128), F32),
        vmem((2, 16, 64, 128)),
        vmem((2, 16, 64, 128)),
        vmem((2, 8, 8, 128), F32),
        vmem((2, 16, 8, 128), F32),
        pltpu.SemaphoreType.DMA((4,)),
        pltpu.SemaphoreType.DMA((2,)),
        pltpu.SemaphoreType.DMA((4,)),
        pltpu.SemaphoreType.DMA((4,)),
        pltpu.SemaphoreType.DMA((4,)),
        pltpu.SemaphoreType.DMA((4,)),
        pltpu.SemaphoreType.DMA((2, 16)),
        pltpu.SemaphoreType.DMA((2, 16)),
        pltpu.SemaphoreType.DMA((2, 16)),
        pltpu.SemaphoreType.DMA((2, 16)),
    ]
    anywhere = pl.BlockSpec(memory_space=pl.ANY)
    in_vmem = pl.BlockSpec(memory_space=pltpu.VMEM)
    features, back, first, second = pl.pallas_call(
        functools.partial(kernel, slabs=slabs, scale=1.0 / math.sqrt(voxels)),
        out_shape=(
            jax.ShapeDtypeStruct(volume.shape, BF16),
            jax.ShapeDtypeStruct(volume.shape, BF16),
            jax.ShapeDtypeStruct((8, 128), F32),
            jax.ShapeDtypeStruct((8, 128), F32),
        ),
        in_specs=[anywhere] * 4,
        out_specs=(anywhere, anywhere, in_vmem, in_vmem),
        scratch_shapes=scratch,
        compiler_params=pltpu.CompilerParams(
            collective_id=0, has_side_effects=True, vmem_limit_bytes=48 * 2**20
        ),
    )(volume, cotangent, first_weight, second_weight)
    return (features, back, first.reshape(-1)[:432], second.reshape(-1)[:432])


def solution(mesh):
    slabs = mesh.shape["slab"]
    voxels = 524288
    split = P("sample", "slab", None, None)
    return jax.shard_map(
        functools.partial(per_device, slabs=slabs, voxels=voxels),
        mesh=mesh,
        in_specs=(split, split, P(), P()),
        out_specs=(split, split, P(("sample", "slab")), P(("sample", "slab"))),
        check_vma=False,
    )
```

profile of v0, /device:TPU:1, one launch (start us, length us, event | category | flops | bytes accessed | tf_op | source)
XLA Modules:
  0.0 51.6 jit_solution(8134110777676846038)
XLA Ops:
  0.6 0.0 copy-start
  0.6 1.0 %copy-done = bf16[3,3,3,64,64]{4,3,2,1,0:T(8,128)(2,1)S(1)} copy-done((bf16[3,3,3,64,64]{4,3,2,1,0:T(8,128)(2,1)S(1)}, bf16[3,3,3,64,64]{4,3,2,1,0:T(8,128)(2,1)}, u32[]{:S(2)}) %copy-start) | copy-done | bytes 221208
  1.6 0.0 copy-start.1
  1.6 1.0 %copy-done.1 = bf16[3,3,3,64,64]{4,3,2,1,0:T(8,128)(2,1)S(1)} copy-done((bf16[3,3,3,64,64]{4,3,2,1,0:T(8,128)(2,1)S(1)}, bf16[3,3,3,64,64]{4,3,2,1,0:T(8,128)(2,1)}, u32[]{:S(2)}) %copy-start.1) | copy-done | bytes 221208
  2.7 0.0 copy-start.2
  2.7 0.9 %copy-done.2 = bf16[1,2,32,2048]{3,2,1,0:T(8,128)(2,1)S(1)} copy-done((bf16[1,2,32,2048]{3,2,1,0:T(8,128)(2,1)S(1)}, bf16[1,2,32,2048]{3,2,1,0:T(8,128)(2,1)}, u32[]{:S(2)}) %copy-start.2) | copy-done | bytes 262168
  3.6 0.0 copy-start.3
  3.6 0.9 %copy-done.3 = bf16[1,2,32,2048]{3,2,1,0:T(8,128)(2,1)S(1)} copy-done((bf16[1,2,32,2048]{3,2,1,0:T(8,128)(2,1)S(1)}, bf16[1,2,32,2048]{3,2,1,0:T(8,128)(2,1)}, u32[]{:S(2)}) %copy-start.3) | copy-done | bytes 262168
  4.6 44.5 %shard_map.75 = (bf16[1,2,32,2048]{3,2,1,0:T(8,128)(2,1)S(1)}, bf16[1,2,32,2048]{3,2,1,0:T(8,128)(2,1)S(1)}, f32[8,128]{1,0:T(8,128)S(1)}, f32[8,128]{1,0:T(8,128)S(1)}) custom-call(bf16[1,2,32,2048]{3,2,1,0:T(8,128)(2,1)S(1)} %copy-done.2, bf16[1,2,32,2048]{3,2,1,0:T(8,128)(2,1)S(1)} %copy-done.3, bf16[3,3,3,64,64]{4,3,2,1,0:T(8,128)(2,1)S(1)} %copy-done, ...), custom_call_target="tpu_custom_call" | custom-call | tf_op jit(solution)/shard_map/pallas_call | solution.py:550
  49.0 0.6 %slice.6 = f32[432]{0:T(512)} slice(f32[1024]{0:T(1024)S(1)} %bitcast.3), slice={[0:432]} | slice | bytes 3456 | tf_op jit(solution)/shard_map/slice | solution.py:565
  49.6 0.6 %slice.7 = f32[432]{0:T(512)} slice(f32[1024]{0:T(1024)S(1)} %bitcast.2), slice={[0:432]} | slice | bytes 3456 | tf_op jit(solution)/shard_map/slice | solution.py:565
  50.2 0.7 %copy.10 = bf16[1,2,32,2048]{3,2,1,0:T(8,128)(2,1)} copy(bf16[1,2,32,2048]{3,2,1,0:T(8,128)(2,1)S(1)} %get-tuple-element.16) | data formatting | bytes 524288
  50.9 0.7 %copy.11 = bf16[1,2,32,2048]{3,2,1,0:T(8,128)(2,1)} copy(bf16[1,2,32,2048]{3,2,1,0:T(8,128)(2,1)S(1)} %get-tuple-element.17) | data formatting | bytes 524288
Async XLA Ops:
  0.6 1.0 %copy-start = (bf16[3,3,3,64,64]{4,3,2,1,0:T(8,128)(2,1)S(1)}, bf16[3,3,3,64,64]{4,3,2,1,0:T(8,128)(2,1)}, u32[]{:S(2)}) copy-start(bf16[3,3,3,64,64]{4,3,2,1,0:T(8,128)(2,1)} %w1_hbm.1) | copy-start | bytes 663556
  1.6 1.0 %copy-start.1 = (bf16[3,3,3,64,64]{4,3,2,1,0:T(8,128)(2,1)S(1)}, bf16[3,3,3,64,64]{4,3,2,1,0:T(8,128)(2,1)}, u32[]{:S(2)}) copy-start(bf16[3,3,3,64,64]{4,3,2,1,0:T(8,128)(2,1)} %w2_hbm.1) | copy-start | bytes 663556
  2.7 0.9 %copy-start.2 = (bf16[1,2,32,2048]{3,2,1,0:T(8,128)(2,1)S(1)}, bf16[1,2,32,2048]{3,2,1,0:T(8,128)(2,1)}, u32[]{:S(2)}) copy-start(bf16[1,2,32,2048]{3,2,1,0:T(8,128)(2,1)} %vol_hbm.1) | copy-start | bytes 786436
  3.6 0.9 %copy-start.3 = (bf16[1,2,32,2048]{3,2,1,0:T(8,128)(2,1)S(1)}, bf16[1,2,32,2048]{3,2,1,0:T(8,128)(2,1)}, u32[]{:S(2)}) copy-start(bf16[1,2,32,2048]{3,2,1,0:T(8,128)(2,1)} %cot_hbm.1) | copy-start | bytes 786436
where the time goes:
time: 51.8 us; the launch traced here: 51.6 us
  Pallas kernels  44.5 us (86%)
  local copies, waits for them, and re-layouts  6.48 us (13%)
  between operations  0.65 us (1%)
    pallas_call x1, Pallas kernels, per_device(): pl.pallas_call(functools.partial(kernel, slabs=slabs, scale=1.0 / math.sq...  44.5 us
    unnamed x10, local copies, waits for them, and re-layouts  5.32 us
    slice x2, local copies, waits for them, and re-layouts, per_device(): return (features, back, first.reshape(-1)[:432], second.reshape(-1)[:432])  1.16 us

commit v1 on v0

--- a/solution.py
+++ b/solution.py
@@ -24,6 +24,10 @@
 
 def dot(a, b):
     return lax.dot_general(a, b, (((1,), (0,)), ((), ())), preferred_element_type=F32)
+
+
+def dot_transposed(a, b):
+    return lax.dot_general(a, b, (((1,), (1,)), ((), ())), preferred_element_type=F32)
 
 
 def sigmoid(v):
@@ -63,36 +67,31 @@
 def expand_weight(weight, forward, backward):
     zero = jnp.zeros((C, C), BF16)
     blank = jnp.zeros((C, 128), BF16)
-
-    def tap(index, carry):
-        kx = index // 3
-        ky = index % 3
-        m = [weight[kx, ky, kz] for kz in range(3)]
-        pair = jnp.concatenate([m[0], m[1]], axis=1).astype(F32).T.astype(BF16)
-        last = jnp.concatenate([m[2], zero], axis=1).astype(F32).T.astype(BF16)
-        n = [pair[:C], pair[C:], last[:C]]
-        cat = lambda a, b: jnp.concatenate([a, b], axis=1)
-        ahead = (cat(m[0], zero), cat(m[1], m[0]), cat(m[2], m[1]), cat(zero, m[2]))
-        back = (cat(zero, n[0]), cat(n[0], n[1]), cat(n[1], n[2]), cat(n[2], zero))
-        for w, offset in enumerate(OFFSETS):
-            there = pl.ds(pl.multiple_of(ky * WINDOW + w * C, C), C)
-            mirrored = pl.ds(pl.multiple_of((2 - ky) * WINDOW + w * C, C), C)
-            for half in range(2):
-                a = offset - 2 * half + 1
-                b = 2 * half - offset + 2
-                cols = slice(128 * half, 128 * half + 128)
-                forward[kx, there, cols] = ahead[a] if 0 <= a < 4 else blank
-                backward[2 - kx, mirrored, cols] = back[b] if 0 <= b < 4 else blank
-        return carry
-
-    lax.fori_loop(0, 9, tap, 0)
-
-
-def convolve(win, first, planes, weight):
+    both = lambda a, b: jnp.concatenate([a, b], axis=1)
+    for kx in range(3):
+        for ky in range(3):
+            m = [weight[kx, ky, kz] for kz in range(3)]
+            tiles = (both(m[0], zero), both(m[1], m[0]), both(m[2], m[1]), both(zero, m[2]))
+            for w, offset in enumerate(OFFSETS):
+                there = slice(ky * WINDOW + w * C, ky * WINDOW + w * C + C)
+                for half in range(2):
+                    a = offset - 2 * half + 1
+                    forward[kx, there, 128 * half : 128 * half + 128] = tiles[a] if 0 <= a < 4 else blank
+            for zi in range(4):
+                for pair in range(3):
+                    start = (2 - ky) * WINDOW + 128 * pair
+                    a = zi - 2 * pair + 1 if pair < 2 else {0: 3, 3: 0}.get(zi, -1)
+                    backward[2 - kx, zi * C : zi * C + C, start : start + 128] = (
+                        tiles[a] if 0 <= a < 4 else blank
+                    )
+
+
+def convolve(win, first, planes, weight, mirrored=False):
+    product = dot_transposed if mirrored else dot
     total = None
     for e in range(3):
         lhs = win[(first + e) * 256 : (first + e + planes) * 256, :]
-        term = dot(lhs, weight[e])
+        term = product(lhs, weight[e])
         total = term if total is None else total + term
     return total
 
@@ -192,11 +191,13 @@
     z = z_hi * 4 + z_lo
 
     def near_partner(r):
-        return (((y + r // 4) % 4) * 2 + z_hi, z_lo * 8 + ((x + r % 4) % 4) * 2 + core)
+        return (lax.rem(y + r // 4, 4) * 2 + z_hi, z_lo * 8 + lax.rem(x + r % 4, 4) * 2 + core)
 
     def far_partner(r):
-        zz = (z + r // 2) % 8
-        return (y * 2 + zz // 4, (zz % 4) * 8 + x * 2 + (core + r % 2) % 2)
+        zz = lax.rem(z + r // 2, 8)
+        return (y * 2 + lax.div(zz, 4), lax.rem(zz, 4) * 8 + x * 2 + lax.rem(core + r % 2, 2))
+
+    alone = pl.when(slab >= 0)
 
     has_low = slab > 0
     has_high = slab < slabs - 1
@@ -213,12 +214,9 @@
     def _():
         pl.semaphore_signal(barrier, inc=1, device_id=high, device_id_type=MESH)
 
-    def greet(r, carry):
+    for r in range(1, 16):
         pl.semaphore_signal(barrier, inc=1, device_id=near_partner(r), device_id_type=MESH)
         pl.semaphore_signal(barrier, inc=1, device_id=far_partner(r), device_id_type=MESH)
-        return carry
-
-    lax.fori_loop(1, 16, greet, 0)
 
     loads = [
         pltpu.make_async_copy(w1_hbm, w1, load_sem.at[0]),
@@ -298,7 +296,10 @@
         lax.fori_loop(0, 2, body, 0)
 
     prepare_pair(vol, win_v, (1, 4))
-    own_pre[...] = convolve(win_v, 1, 2, ahead1)
+    @alone
+    def _():
+        own_pre[...] = convolve(win_v, 1, 2, ahead1)
+
 
     @pl.when(has_low)
     def _():
@@ -309,8 +310,11 @@
         to_low(1).wait_recv()
 
     prepare_pair(vol, win_v, (0, 5))
-    pre[0:256, :] = convolve(win_v, 0, 1, ahead1)
-    pre[256:512, :] = convolve(win_v, 3, 1, ahead1)
+    @alone
+    def _():
+        pre[0:256, :] = convolve(win_v, 0, 1, ahead1)
+        pre[256:512, :] = convolve(win_v, 3, 1, ahead1)
+
 
     def hide(source, at, plane, keep):
         for j in range(QUADS):
@@ -326,7 +330,10 @@
     hide(pre, 256, 3, has_high)
     prepare_pair(hid, win_h, (0, 1))
     prepare_pair(hid, win_h, (2, 3))
-    acc[...] = convolve(win_h, 0, 2, ahead2)
+    @alone
+    def _():
+        acc[...] = convolve(win_h, 0, 2, ahead2)
+
 
     loads[3].wait()
 
@@ -376,7 +383,7 @@
     me_near = y * 4 + x
 
     def near_copy(which, r):
-        other = ((y + r // 4) % 4) * 4 + (x + r % 4) % 4
+        other = lax.rem(y + r // 4, 4) * 4 + lax.rem(x + r % 4, 4)
         return pltpu.make_async_remote_copy(
             near.at[which, other],
             near_in.at[which, r],
@@ -387,17 +394,14 @@
         )
 
     def far_copy(which, r):
-        zz = (z + r // 2) % 8
+        zz = lax.rem(z + r // 2, 8)
         return pltpu.make_async_remote_copy(
             far.at[which, zz], far_in.at[which, r], far_send.at[which, r], far_recv.at[which, r], far_partner(r), MESH
         )
 
     def each(copy, what, which):
-        def body(r, carry):
+        for r in range(1, 16):
             getattr(copy(which, r), what)()
-            return carry
-
-        lax.fori_loop(1, 16, body, 0)
 
     def send_near(which):
         def row(yy, carry):
@@ -449,7 +453,10 @@
 
     receive_halos(g2, 0)
     prepare_pair(g2, win_g2, (0, 3))
-    acc[...] = convolve(win_g2, 0, 2, back2)
+    @alone
+    def _():
+        acc[...] = convolve(win_g2, 0, 2, back2, True)
+
 
     def first_stage(plane, carry):
         for j in range(QUADS):
@@ -471,7 +478,10 @@
 
     receive_halos(g1, 1)
     prepare_pair(g1, win_g1, (0, 3))
-    acc[...] = convolve(win_g1, 0, 2, back1)
+    @alone
+    def _():
+        acc[...] = convolve(win_g1, 0, 2, back1, True)
+
     for plane in range(2):
         for j in range(QUADS):
             at = (plane * QUADS + j) * CELLS
@@ -502,6 +512,15 @@
         each(far_copy, "wait_send", which)
     features_store.wait()
     back_store.wait()
+
+
+def hand_over(feat_in, back_in, first_in, second_in, feat_out, back_out, first_out, second_out):
+    feat_out[...] = feat_in[...]
+    back_out[...] = back_in[...]
+    for source, target in ((first_in, first_out), (second_in, second_out)):
+        for row in range(3):
+            target[pl.ds(row * 128, 128)] = source[row]
+        target[pl.ds(384, 48)] = source[3, :48]
 
 
 def per_device(volume, cotangent, first_weight, second_weight, *, slabs, voxels):
@@ -512,9 +531,9 @@
         vmem((3, 3, 3, C, C)),
         vmem((3, 3, 3, C, C)),
         vmem((3, WIDE, 256)),
+        vmem((3, 256, WIDE)),
         vmem((3, WIDE, 256)),
-        vmem((3, WIDE, 256)),
-        vmem((3, WIDE, 256)),
+        vmem((3, 256, WIDE)),
         vmem((6 * 256, WIDE)),
         vmem((4 * 256, WIDE)),
         vmem((4 * 256, WIDE)),
@@ -559,10 +578,20 @@
         out_specs=(anywhere, anywhere, in_vmem, in_vmem),
         scratch_shapes=scratch,
         compiler_params=pltpu.CompilerParams(
-            collective_id=0, has_side_effects=True, vmem_limit_bytes=48 * 2**20
+            collective_id=0, has_side_effects=True, vmem_limit_bytes=63 * 2**20
         ),
     )(volume, cotangent, first_weight, second_weight)
-    return (features, back, first.reshape(-1)[:432], second.reshape(-1)[:432])
+    return pl.pallas_call(
+        hand_over,
+        out_shape=(
+            jax.ShapeDtypeStruct(volume.shape, BF16),
+            jax.ShapeDtypeStruct(volume.shape, BF16),
+            jax.ShapeDtypeStruct((432,), F32),
+            jax.ShapeDtypeStruct((432,), F32),
+        ),
+        in_specs=[in_vmem] * 4,
+        out_specs=(in_vmem,) * 4,
+    )(features, back, first, second)
 
 
 def solution(mesh):

time: 51.8 us -> 43.5 us (0.84)
  local copies, waits for them, and re-layouts: 6.48 us -> 0 us
  Pallas kernels: 44.5 us -> 42.7 us
    unnamed x10 -> x0, local copies, waits for them, and re-layouts: 5.32 us -> none
    pallas_call x1, Pallas kernels: 44.5 us -> 40.9 us  [per_device(): pl.pallas_call(functools.partial(kernel, slabs=slabs, scale=1.0 / math.sq...]
    pallas_call x0 -> x1, Pallas kernels: none -> 1.85 us  [per_device(): pl.pallas_call(hand_over, out_shape=(jax.ShapeDtypeStruct(volume.shape, B...]
    slice x2 -> x0, local copies, waits for them, and re-layouts: 1.16 us -> none  [per_device(): return (features, back, first.reshape(-1)[:432], second.reshape(-1)[:432])]
where the time goes in v1:
time: 43.5 us; the launch traced here: 43.4 us
  Pallas kernels  42.7 us (98%)
  between operations  0.64 us (1%)
    pallas_call x1, Pallas kernels, per_device(): pl.pallas_call(functools.partial(kernel, slabs=slabs, scale=1.0 / math.sq...  40.9 us
    pallas_call x1, Pallas kernels, per_device(): pl.pallas_call(hand_over, out_shape=(jax.ShapeDtypeStruct(volume.shape, B...  1.85 us

profile of v1, /device:TPU:1, one launch (start us, length us, event | category | flops | bytes accessed | tf_op | source)
XLA Modules:
  0.0 43.4 jit_solution(10759910768243602225)
XLA Ops:
  0.6 40.9 %shard_map.75 = (bf16[1,2,32,2048]{3,2,1,0:T(8,128)(2,1)}, bf16[1,2,32,2048]{3,2,1,0:T(8,128)(2,1)}, f32[8,128]{1,0:T(8,128)}, f32[8,128]{1,0:T(8,128)}) custom-call(bf16[1,2,32,2048]{3,2,1,0:T(8,128)(2,1)} %vol_hbm.1, bf16[1,2,32,2048]{3,2,1,0:T(8,128)(2,1)} %cot_hbm.1, bf16[3,3,3,64,64]{4,3,2,1,0:T(8,128)(2,1)} %w1_hbm.1, bf16[3,3,3,64,64]{4,3,2,1,0:T(8,128)(2,1)} %w2_hbm.1), custom_call_target="tpu_custom_call" | custom-call | tf_op jit(solution)/shard_map/pallas_call | solution.py:569
  41.5 1.8 %shard_map.76 = (bf16[1,2,32,2048]{3,2,1,0:T(8,128)(2,1)}, bf16[1,2,32,2048]{3,2,1,0:T(8,128)(2,1)}, f32[432]{0:T(512)}, f32[432]{0:T(512)}) custom-call(bf16[1,2,32,2048]{3,2,1,0:T(8,128)(2,1)} %get-tuple-element.8.feat_in, bf16[1,2,32,2048]{3,2,1,0:T(8,128)(2,1)} %get-tuple-element.9.back_in, f32[8,128]{1,0:T(8,128)} %get-tuple-element.10.first_in, ...), custom_call_target="tpu_custom_call" | custom-call | tf_op jit(solution)/shard_map/pallas_call | solution.py:584

commit v2 on v1

--- a/solution.py
+++ b/solution.py
@@ -86,25 +86,30 @@
                     )
 
 
-def convolve(win, first, planes, weight, mirrored=False):
-    product = dot_transposed if mirrored else dot
-    total = None
+def planes_of(win, slot, count=1):
+    return win[slot * 256 : (slot + count) * 256, :]
+
+
+def convolve_own(win, slot, weight, out, product=dot):
+    middle = product(planes_of(win, slot, 2), weight[1])
+    out[0:256, :] = middle[:256] + product(planes_of(win, slot + 1), weight[2])
+    out[256:512, :] = middle[256:] + product(planes_of(win, slot), weight[0])
+
+
+def convolve_outer(win, slot, weight, out, product=dot):
+    out[0:256, :] += product(planes_of(win, slot - 1), weight[0])
+    out[256:512, :] += product(planes_of(win, slot + 2), weight[2])
+
+
+def kernel_gradient(flipped, win, first, product, flat, ready):
+    low_half = lax.broadcasted_iota(jnp.int32, (32, 128), 1) < C
+
     for e in range(3):
-        lhs = win[(first + e) * 256 : (first + e + planes) * 256, :]
-        term = product(lhs, weight[e])
-        total = term if total is None else total + term
-    return total
-
-
-def kernel_gradient(flipped, win, first, product, flat):
-    whole = dot(flipped[0:768], win[first * 256 : first * 256 + 256, :]) + dot(
-        flipped[256:1024], win[first * 256 + 256 : first * 256 + 512, :]
-    )
-    for tile in range(9):
-        product[tile] = whole[:, tile * 128 : tile * 128 + 128]
-    low_half = lax.broadcasted_iota(jnp.int32, (32, 128), 1) < C
-
-    for e in range(3):
+        whole = dot(planes_of(flipped, e), planes_of(win, first)) + dot(
+            planes_of(flipped, e + 1), planes_of(win, first + 1)
+        )
+        for tile in range(9):
+            product[tile, e * 256 : e * 256 + 256, :] = whole[:, tile * 128 : tile * 128 + 128]
         for ky in range(3):
             column = (2 - ky) * 3
 
@@ -132,6 +137,7 @@
                 crossed = jnp.where(low_half, low1, high0)
                 tap = (e * 3 + ky) * 3 + kz
                 flat[tap * 32 : tap * 32 + 32, :] = straight + pltpu.roll(crossed, C, 1)
+        ready(e)
 
 
 def kernel(
@@ -155,7 +161,8 @@
     win_h,
     win_g2,
     win_g1,
-    flipped,
+    flipped_v,
+    flipped_h,
     hid,
     g2,
     g1,
@@ -271,22 +278,6 @@
                 buffer[slot] = no_plane
 
     flat[TAPROWS : TAPROWS + 8, :] = jnp.zeros((8, 128), F32)
-    loads[0].wait()
-    expand_weight(w1, ahead1, back1)
-    loads[1].wait()
-    prepare(vol, 2, win_v, 2)
-    prepare(vol, 3, win_v, 3)
-    loads[2].wait()
-    expand_weight(w2, ahead2, back2)
-
-    @pl.when(has_low)
-    def _():
-        to_high(1).wait_recv()
-
-    @pl.when(has_high)
-    def _():
-        to_low(0).wait_recv()
-
     def prepare_pair(src, win, slots):
         def body(i, carry):
             slot = slots[0] + i * (slots[1] - slots[0])
@@ -294,27 +285,6 @@
             return carry
 
         lax.fori_loop(0, 2, body, 0)
-
-    prepare_pair(vol, win_v, (1, 4))
-    @alone
-    def _():
-        own_pre[...] = convolve(win_v, 1, 2, ahead1)
-
-
-    @pl.when(has_low)
-    def _():
-        to_high(0).wait_recv()
-
-    @pl.when(has_high)
-    def _():
-        to_low(1).wait_recv()
-
-    prepare_pair(vol, win_v, (0, 5))
-    @alone
-    def _():
-        pre[0:256, :] = convolve(win_v, 0, 1, ahead1)
-        pre[256:512, :] = convolve(win_v, 3, 1, ahead1)
-
 
     def hide(source, at, plane, keep):
         for j in range(QUADS):
@@ -324,18 +294,82 @@
                 value = jnp.where(keep, value, 0.0)
             hid[plane, :, j * 256 : j * 256 + 256] = value.astype(BF16)
 
-    hide(pre, 0, 0, has_low)
+    loads[0].wait()
+    expand_weight(w1, ahead1, back1)
+    loads[1].wait()
+    prepare_pair(vol, win_v, (2, 3))
+
+    @alone
+    def _():
+        convolve_own(win_v, 2, ahead1, own_pre)
+        pre[0:256, :] = dot(planes_of(win_v, 2), ahead1[2])
+        pre[256:512, :] = dot(planes_of(win_v, 3), ahead1[0])
+
+    loads[2].wait()
+    expand_weight(w2, ahead2, back2)
+
+    @pl.when(has_low)
+    def _():
+        to_high(1).wait_recv()
+
+    @pl.when(has_high)
+    def _():
+        to_low(0).wait_recv()
+
+    prepare_pair(vol, win_v, (1, 4))
+
+    @alone
+    def _():
+        convolve_outer(win_v, 2, ahead1, own_pre)
+        pre[0:256, :] += dot(planes_of(win_v, 1), ahead1[1])
+        pre[256:512, :] += dot(planes_of(win_v, 4), ahead1[1])
+
     hide(own_pre, 0, 1, None)
     hide(own_pre, 256, 2, None)
+    prepare_pair(hid, win_h, (1, 2))
+
+    @alone
+    def _():
+        convolve_own(win_h, 1, ahead2, acc)
+
+    @pl.when(has_low)
+    def _():
+        to_high(0).wait_recv()
+
+    @pl.when(has_high)
+    def _():
+        to_low(1).wait_recv()
+
+    prepare_pair(vol, win_v, (0, 5))
+
+    @alone
+    def _():
+        pre[0:256, :] += dot(planes_of(win_v, 0), ahead1[0])
+        pre[256:512, :] += dot(planes_of(win_v, 5), ahead1[2])
+
+    hide(pre, 0, 0, has_low)
     hide(pre, 256, 3, has_high)
-    prepare_pair(hid, win_h, (0, 1))
-    prepare_pair(hid, win_h, (2, 3))
-    @alone
-    def _():
-        acc[...] = convolve(win_h, 0, 2, ahead2)
-
+    prepare_pair(hid, win_h, (0, 3))
+
+    @alone
+    def _():
+        convolve_outer(win_h, 1, ahead2, acc)
 
     loads[3].wait()
+
+    def halo(buffer, which, side):
+        if side == 0:
+            return pltpu.make_async_remote_copy(
+                buffer.at[1], buffer.at[3], g_send.at[2 * which], g_recv.at[2 * which], low, MESH
+            )
+        return pltpu.make_async_remote_copy(
+            buffer.at[2], buffer.at[0], g_send.at[2 * which + 1], g_recv.at[2 * which + 1], high, MESH
+        )
+
+    def send_halo(buffer, which, side):
+        @pl.when(has_high if side else has_low)
+        def _():
+            halo(buffer, which, side).start()
 
     def second_stage(plane, carry):
         for j in range(QUADS):
@@ -347,25 +381,10 @@
             g2[plane + 1, :, cols] = (cot[plane, :, cols].astype(F32) * slope).astype(BF16)
         return carry
 
-    lax.fori_loop(0, 2, second_stage, 0)
-
-    def halo(buffer, which, side):
-        if side == 0:
-            return pltpu.make_async_remote_copy(
-                buffer.at[1], buffer.at[3], g_send.at[2 * which], g_recv.at[2 * which], low, MESH
-            )
-        return pltpu.make_async_remote_copy(
-            buffer.at[2], buffer.at[0], g_send.at[2 * which + 1], g_recv.at[2 * which + 1], high, MESH
-        )
-
-    def send_halos(buffer, which):
-        @pl.when(has_low)
-        def _():
-            halo(buffer, which, 0).start()
-
-        @pl.when(has_high)
-        def _():
-            halo(buffer, which, 1).start()
+    second_stage(0, 0)
+    send_halo(g2, 0, 0)
+    second_stage(1, 0)
+    send_halo(g2, 0, 1)
 
     def receive_halos(buffer, which):
         @pl.when(has_high)
@@ -376,7 +395,6 @@
         def _():
             halo(buffer, which, 1).wait_recv()
 
-    send_halos(g2, 0)
     features_store = pltpu.make_async_copy(feat, feat_hbm.at[0], store_sem.at[0])
     features_store.start()
 
@@ -403,17 +421,31 @@
         for r in range(1, 16):
             getattr(copy(which, r), what)()
 
-    def send_near(which):
-        def row(yy, carry):
-            for xx in range(4):
-                for pair in range(4):
-                    starts = [yy * 216 + (2 * pair + i) * 27 + (27 * xx) // 4 for i in range(2)]
-                    both = jnp.concatenate([flat[pl.ds(s, 8), :] for s in starts], axis=0)
-                    near[which, yy * 4 + xx, 16 * pair : 16 * pair + 16, :] = both.astype(BF16)
-            return carry
-
-        lax.fori_loop(0, 4, row, 0)
-        each(near_copy, "start", which)
+    def send_near(which, e):
+        for yy in (0,), (1,), (2, 3):
+            if yy[0] != e:
+                continue
+            for to in yy:
+                away = lax.rem(to - y + 4, 4)
+                for xx in range(4):
+                    for pair in range(4):
+                        starts = [to * 216 + (2 * pair + i) * 27 + (27 * xx) // 4 for i in range(2)]
+                        both = jnp.concatenate([flat[pl.ds(s, 8), :] for s in starts], axis=0)
+                        near[which, to * 4 + xx, 16 * pair : 16 * pair + 16, :] = both.astype(BF16)
+                for rx in range(4):
+                    other = lax.rem(x + rx, 4)
+                    copy = pltpu.make_async_remote_copy(
+                        near.at[which, to * 4 + other],
+                        near_in.at[which, away * 4 + rx],
+                        near_send.at[which, away * 4 + rx],
+                        near_recv.at[which, away * 4 + rx],
+                        (to * 2 + z_hi, z_lo * 8 + other * 2 + core),
+                        MESH,
+                    )
+                    if rx:
+                        copy.start()
+                    else:
+                        pl.when(away != 0)(copy.start)
 
     def send_far(which):
         each(near_copy, "wait_recv", which)
@@ -440,22 +472,26 @@
 
     prepare_pair(g2, win_g2, (1, 2))
 
-    def flip_planes(win, first):
+    def flip_planes(win, first, out):
         def body(i, carry):
-            transpose_plane(win, first + i, flipped, i)
+            transpose_plane(win, first + i, out, i)
             return carry
 
         lax.fori_loop(0, 4, body, 0)
 
-    flip_planes(win_h, 0)
-    kernel_gradient(flipped, win_g2, 1, product, flat)
-    send_near(1)
+    flip_planes(win_h, 0, flipped_h)
+    kernel_gradient(flipped_h, win_g2, 1, product, flat, functools.partial(send_near, 1))
+    flip_planes(win_v, 1, flipped_v)
+
+    @alone
+    def _():
+        convolve_own(win_g2, 1, back2, acc, dot_transposed)
 
     receive_halos(g2, 0)
     prepare_pair(g2, win_g2, (0, 3))
     @alone
     def _():
-        acc[...] = convolve(win_g2, 0, 2, back2, True)
+        convolve_outer(win_g2, 1, back2, acc, dot_transposed)
 
 
     def first_stage(plane, carry):
@@ -467,20 +503,25 @@
             g1[plane + 1, :, j * 256 : j * 256 + 256] = (acc[at, :] * slope).astype(BF16)
         return carry
 
-    lax.fori_loop(0, 2, first_stage, 0)
-    send_halos(g1, 1)
+    first_stage(0, 0)
+    send_halo(g1, 1, 0)
+    first_stage(1, 0)
+    send_halo(g1, 1, 1)
 
     prepare_pair(g1, win_g1, (1, 2))
-    flip_planes(win_v, 1)
-    kernel_gradient(flipped, win_g1, 1, product, flat)
-    send_near(0)
+    kernel_gradient(flipped_v, win_g1, 1, product, flat, functools.partial(send_near, 0))
+
+    @alone
+    def _():
+        convolve_own(win_g1, 1, back1, acc, dot_transposed)
+
     send_far(1)
 
     receive_halos(g1, 1)
     prepare_pair(g1, win_g1, (0, 3))
     @alone
     def _():
-        acc[...] = convolve(win_g1, 0, 2, back1, True)
+        convolve_outer(win_g1, 1, back1, acc, dot_transposed)
 
     for plane in range(2):
         for j in range(QUADS):
@@ -538,6 +579,7 @@
         vmem((4 * 256, WIDE)),
         vmem((4 * 256, WIDE)),
         vmem((4 * 256, WIDE)),
+        vmem((1024, 256)),
         vmem((1024, 256)),
         vmem((4, CELLS, MERGED)),
         vmem((4, CELLS, MERGED)),

time: 43.5 us -> 41 us (0.943)
  Pallas kernels: 42.7 us -> 40.2 us
    pallas_call x1, Pallas kernels: 40.9 us -> 38.4 us  [per_device(): pl.pallas_call(functools.partial(kernel, slabs=slabs, scale=1.0 / math.sq...]
where the time goes in v2:
time: 41 us; the launch traced here: 40.8 us
  Pallas kernels  40.2 us (98%)
  between operations  0.64 us (2%)
    pallas_call x1, Pallas kernels, per_device(): pl.pallas_call(functools.partial(kernel, slabs=slabs, scale=1.0 / math.sq...  38.4 us
    pallas_call x1, Pallas kernels, per_device(): pl.pallas_call(hand_over, out_shape=(jax.ShapeDtypeStruct(volume.shape, B...  1.85 us

profile of v2, /device:TPU:1, one launch (start us, length us, event | category | flops | bytes accessed | tf_op | source)
XLA Modules:
  0.0 40.8 jit_solution(5764670669976483608)
XLA Ops:
  0.6 38.4 %shard_map.75 = (bf16[1,2,32,2048]{3,2,1,0:T(8,128)(2,1)}, bf16[1,2,32,2048]{3,2,1,0:T(8,128)(2,1)}, f32[8,128]{1,0:T(8,128)}, f32[8,128]{1,0:T(8,128)}) custom-call(bf16[1,2,32,2048]{3,2,1,0:T(8,128)(2,1)} %vol_hbm.1, bf16[1,2,32,2048]{3,2,1,0:T(8,128)(2,1)} %cot_hbm.1, bf16[3,3,3,64,64]{4,3,2,1,0:T(8,128)(2,1)} %w1_hbm.1, bf16[3,3,3,64,64]{4,3,2,1,0:T(8,128)(2,1)} %w2_hbm.1), custom_call_target="tpu_custom_call" | custom-call | tf_op jit(solution)/shard_map/pallas_call | solution.py:611
  39.0 1.8 %shard_map.76 = (bf16[1,2,32,2048]{3,2,1,0:T(8,128)(2,1)}, bf16[1,2,32,2048]{3,2,1,0:T(8,128)(2,1)}, f32[432]{0:T(512)}, f32[432]{0:T(512)}) custom-call(bf16[1,2,32,2048]{3,2,1,0:T(8,128)(2,1)} %get-tuple-element.8.feat_in, bf16[1,2,32,2048]{3,2,1,0:T(8,128)(2,1)} %get-tuple-element.9.back_in, f32[8,128]{1,0:T(8,128)} %get-tuple-element.10.first_in, ...), custom_call_target="tpu_custom_call" | custom-call | tf_op jit(solution)/shard_map/pallas_call | solution.py:626

commit v3 on v2

--- a/solution.py
+++ b/solution.py
@@ -87,7 +87,9 @@
 
 
 def planes_of(win, slot, count=1):
-    return win[slot * 256 : (slot + count) * 256, :]
+    if isinstance(slot, int):
+        return win[slot * 256 : (slot + count) * 256, :]
+    return win[pl.ds(pl.multiple_of(slot * 256, 256), count * 256), :]
 
 
 def convolve_own(win, slot, weight, out, product=dot):
@@ -96,9 +98,9 @@
     out[256:512, :] = middle[256:] + product(planes_of(win, slot), weight[0])
 
 
-def convolve_outer(win, slot, weight, out, product=dot):
-    out[0:256, :] += product(planes_of(win, slot - 1), weight[0])
-    out[256:512, :] += product(planes_of(win, slot + 2), weight[2])
+def add_outer(win, slot, weight, out, side, product=dot):
+    at = pl.ds(pl.multiple_of(side * 256, 256), 256)
+    out[at, :] += product(planes_of(win, slot), weight[2 * side])
 
 
 def kernel_gradient(flipped, win, first, product, flat, ready):
@@ -308,52 +310,51 @@
     loads[2].wait()
     expand_weight(w2, ahead2, back2)
 
-    @pl.when(has_low)
-    def _():
-        to_high(1).wait_recv()
-
-    @pl.when(has_high)
-    def _():
-        to_low(0).wait_recv()
-
-    prepare_pair(vol, win_v, (1, 4))
+    def on_side(side, act_low, act_high):
+        pl.when(jnp.logical_and(side == 0, has_low))(act_low)
+        pl.when(jnp.logical_and(side == 1, has_high))(act_high)
+
+    def side_of(i):
+        return lax.rem(1 - core + i, 2)
+
+    def volume_side(i, carry):
+        side = side_of(i)
+        on_side(side, lambda: to_high(1).wait_recv(), lambda: to_low(0).wait_recv())
+        slot = 1 + 3 * side
+        prepare(vol, slot, win_v, slot)
+
+        @alone
+        def _():
+            add_outer(win_v, slot, ahead1, own_pre, side)
+            at = pl.ds(pl.multiple_of(side * 256, 256), 256)
+            pre[at, :] += dot(planes_of(win_v, slot), ahead1[1])
+
+        hide(own_pre, side * 256, 1 + side, None)
+        prepare(hid, 1 + side, win_h, 1 + side)
+
+        @pl.when(i == 1)
+        def _():
+            convolve_own(win_h, 1, ahead2, acc)
+            add_outer(win_h, 3 * (1 - side), ahead2, acc, 1 - side)
+
+        on_side(side, lambda: to_high(0).wait_recv(), lambda: to_low(1).wait_recv())
+        prepare(vol, 5 * side, win_v, 5 * side)
+
+        @alone
+        def _():
+            add_outer(win_v, 5 * side, ahead1, pre, side)
+
+        inside = jnp.logical_or(jnp.logical_and(side == 0, has_low), jnp.logical_and(side == 1, has_high))
+        hide(pre, side * 256, 3 * side, inside)
+        prepare(hid, 3 * side, win_h, 3 * side)
+        return carry
+
+    lax.fori_loop(0, 2, volume_side, 0)
 
     @alone
     def _():
-        convolve_outer(win_v, 2, ahead1, own_pre)
-        pre[0:256, :] += dot(planes_of(win_v, 1), ahead1[1])
-        pre[256:512, :] += dot(planes_of(win_v, 4), ahead1[1])
-
-    hide(own_pre, 0, 1, None)
-    hide(own_pre, 256, 2, None)
-    prepare_pair(hid, win_h, (1, 2))
-
-    @alone
-    def _():
-        convolve_own(win_h, 1, ahead2, acc)
-
-    @pl.when(has_low)
-    def _():
-        to_high(0).wait_recv()
-
-    @pl.when(has_high)
-    def _():
-        to_low(1).wait_recv()
-
-    prepare_pair(vol, win_v, (0, 5))
-
-    @alone
-    def _():
-        pre[0:256, :] += dot(planes_of(win_v, 0), ahead1[0])
-        pre[256:512, :] += dot(planes_of(win_v, 5), ahead1[2])
-
-    hide(pre, 0, 0, has_low)
-    hide(pre, 256, 3, has_high)
-    prepare_pair(hid, win_h, (0, 3))
-
-    @alone
-    def _():
-        convolve_outer(win_h, 1, ahead2, acc)
+        side = side_of(1)
+        add_outer(win_h, 3 * side, ahead2, acc, side)
 
     loads[3].wait()
 
@@ -385,15 +386,6 @@
     send_halo(g2, 0, 0)
     second_stage(1, 0)
     send_halo(g2, 0, 1)
-
-    def receive_halos(buffer, which):
-        @pl.when(has_high)
-        def _():
-            halo(buffer, which, 0).wait_recv()
-
-        @pl.when(has_low)
-        def _():
-            halo(buffer, which, 1).wait_recv()
 
     features_store = pltpu.make_async_copy(feat, feat_hbm.at[0], store_sem.at[0])
     features_store.start()
@@ -487,13 +479,6 @@
     def _():
         convolve_own(win_g2, 1, back2, acc, dot_transposed)
 
-    receive_halos(g2, 0)
-    prepare_pair(g2, win_g2, (0, 3))
-    @alone
-    def _():
-        convolve_outer(win_g2, 1, back2, acc, dot_transposed)
-
-
     def first_stage(plane, carry):
         for j in range(QUADS):
             at = pl.ds(pl.multiple_of(plane * 256 + j * CELLS, CELLS), CELLS)
@@ -503,12 +488,28 @@
             g1[plane + 1, :, j * 256 : j * 256 + 256] = (acc[at, :] * slope).astype(BF16)
         return carry
 
-    first_stage(0, 0)
-    send_halo(g1, 1, 0)
-    first_stage(1, 0)
-    send_halo(g1, 1, 1)
-
-    prepare_pair(g1, win_g1, (1, 2))
+    def receive_side(buffer, which, side):
+        on_side(
+            side,
+            lambda: halo(buffer, which, 1).wait_recv(),
+            lambda: halo(buffer, which, 0).wait_recv(),
+        )
+
+    def g2_side(i, carry):
+        side = side_of(i)
+        receive_side(g2, 0, side)
+        prepare(g2, 3 * side, win_g2, 3 * side)
+
+        @alone
+        def _():
+            add_outer(win_g2, 3 * side, back2, acc, side, dot_transposed)
+
+        first_stage(side, 0)
+        on_side(side, lambda: halo(g1, 1, 0).start(), lambda: halo(g1, 1, 1).start())
+        prepare(g1, 1 + side, win_g1, 1 + side)
+        return carry
+
+    lax.fori_loop(0, 2, g2_side, 0)
     kernel_gradient(flipped_v, win_g1, 1, product, flat, functools.partial(send_near, 0))
 
     @alone
@@ -517,12 +518,18 @@
 
     send_far(1)
 
-    receive_halos(g1, 1)
-    prepare_pair(g1, win_g1, (0, 3))
-    @alone
-    def _():
-        convolve_outer(win_g1, 1, back1, acc, dot_transposed)
-
+    def g1_side(i, carry):
+        side = side_of(i)
+        receive_side(g1, 1, side)
+        prepare(g1, 3 * side, win_g1, 3 * side)
+
+        @alone
+        def _():
+            add_outer(win_g1, 3 * side, back1, acc, side, dot_transposed)
+
+        return carry
+
+    lax.fori_loop(0, 2, g1_side, 0)
     for plane in range(2):
         for j in range(QUADS):
             at = (plane * QUADS + j) * CELLS

time: 41 us -> 39.5 us (0.963)
  Pallas kernels: 40.2 us -> 38.8 us
    pallas_call x1, Pallas kernels: 38.4 us -> 36.9 us  [per_device(): pl.pallas_call(functools.partial(kernel, slabs=slabs, scale=1.0 / math.sq...]
where the time goes in v3:
time: 39.5 us; the launch traced here: 39.4 us
  Pallas kernels  38.8 us (98%)
  between operations  0.64 us (2%)
    pallas_call x1, Pallas kernels, per_device(): pl.pallas_call(functools.partial(kernel, slabs=slabs, scale=1.0 / math.sq...  36.9 us
    pallas_call x1, Pallas kernels, per_device(): pl.pallas_call(hand_over, out_shape=(jax.ShapeDtypeStruct(volume.shape, B...  1.85 us

profile of v3, /device:TPU:1, one launch (start us, length us, event | category | flops | bytes accessed | tf_op | source)
XLA Modules:
  0.0 39.4 jit_solution(11974438661911081332)
XLA Ops:
  0.6 36.9 %shard_map.75 = (bf16[1,2,32,2048]{3,2,1,0:T(8,128)(2,1)}, bf16[1,2,32,2048]{3,2,1,0:T(8,128)(2,1)}, f32[8,128]{1,0:T(8,128)}, f32[8,128]{1,0:T(8,128)}) custom-call(bf16[1,2,32,2048]{3,2,1,0:T(8,128)(2,1)} %vol_hbm.1, bf16[1,2,32,2048]{3,2,1,0:T(8,128)(2,1)} %cot_hbm.1, bf16[3,3,3,64,64]{4,3,2,1,0:T(8,128)(2,1)} %w1_hbm.1, bf16[3,3,3,64,64]{4,3,2,1,0:T(8,128)(2,1)} %w2_hbm.1), custom_call_target="tpu_custom_call" | custom-call | tf_op jit(solution)/shard_map/pallas_call | solution.py:618
  37.6 1.8 %shard_map.76 = (bf16[1,2,32,2048]{3,2,1,0:T(8,128)(2,1)}, bf16[1,2,32,2048]{3,2,1,0:T(8,128)(2,1)}, f32[432]{0:T(512)}, f32[432]{0:T(512)}) custom-call(bf16[1,2,32,2048]{3,2,1,0:T(8,128)(2,1)} %get-tuple-element.8.feat_in, bf16[1,2,32,2048]{3,2,1,0:T(8,128)(2,1)} %get-tuple-element.9.back_in, f32[8,128]{1,0:T(8,128)} %get-tuple-element.10.first_in, ...), custom_call_target="tpu_custom_call" | custom-call | tf_op jit(solution)/shard_map/pallas_call | solution.py:633

commit v4 on v3

--- a/solution.py
+++ b/solution.py
@@ -107,9 +107,8 @@
     low_half = lax.broadcasted_iota(jnp.int32, (32, 128), 1) < C
 
     for e in range(3):
-        whole = dot(planes_of(flipped, e), planes_of(win, first)) + dot(
-            planes_of(flipped, e + 1), planes_of(win, first + 1)
-        )
+        pair = jnp.concatenate([planes_of(flipped, e), planes_of(flipped, e + 1)], axis=1)
+        whole = dot(pair, planes_of(win, first, 2))
         for tile in range(9):
             product[tile, e * 256 : e * 256 + 256, :] = whole[:, tile * 128 : tile * 128 + 128]
         for ky in range(3):
@@ -215,6 +214,22 @@
 
     barrier = pltpu.get_barrier_semaphore()
 
+    def near_hops(r):
+        return min(r // 4, 4 - r // 4) + min(r % 4, 4 - r % 4)
+
+    def far_hops(r):
+        return min(r // 2, 8 - r // 2)
+
+    def greet(least, most):
+        for hops in range(most, least - 1, -1):
+            for r in range(1, 16):
+                if near_hops(r) == hops:
+                    pl.semaphore_signal(barrier, inc=1, device_id=near_partner(r), device_id_type=MESH)
+                if far_hops(r) == hops:
+                    pl.semaphore_signal(barrier, inc=1, device_id=far_partner(r), device_id_type=MESH)
+
+    greet(3, 4)
+
     @pl.when(has_low)
     def _():
         pl.semaphore_signal(barrier, inc=1, device_id=low, device_id_type=MESH)
@@ -223,9 +238,7 @@
     def _():
         pl.semaphore_signal(barrier, inc=1, device_id=high, device_id_type=MESH)
 
-    for r in range(1, 16):
-        pl.semaphore_signal(barrier, inc=1, device_id=near_partner(r), device_id_type=MESH)
-        pl.semaphore_signal(barrier, inc=1, device_id=far_partner(r), device_id_type=MESH)
+    greet(0, 2)
 
     loads = [
         pltpu.make_async_copy(w1_hbm, w1, load_sem.at[0]),
@@ -249,21 +262,18 @@
             vol_hbm.at[0, plane], vol.at[plane], vol_send.at[2 + plane], vol_recv.at[plane], high, MESH
         )
 
-    @pl.when(has_low)
-    def _():
-        to_low(0).start()
-
-    @pl.when(has_high)
-    def _():
-        to_high(1).start()
-
-    @pl.when(has_low)
-    def _():
-        to_low(1).start()
-
-    @pl.when(has_high)
-    def _():
-        to_high(0).start()
+    def on_side(side, act_low, act_high):
+        pl.when(jnp.logical_and(side == 0, has_low))(act_low)
+        pl.when(jnp.logical_and(side == 1, has_high))(act_high)
+
+    def side_of(i):
+        return lax.rem(1 - core + i, 2)
+
+    over_link, on_chip = side_of(1), side_of(0)
+    on_side(over_link, lambda: to_low(0).start(), lambda: to_high(1).start())
+    on_side(on_chip, lambda: to_low(0).start(), lambda: to_high(1).start())
+    on_side(over_link, lambda: to_low(1).start(), lambda: to_high(0).start())
+    on_side(on_chip, lambda: to_low(1).start(), lambda: to_high(0).start())
 
     no_plane = jnp.zeros((CELLS, MERGED), BF16)
 
@@ -301,6 +311,12 @@
     loads[1].wait()
     prepare_pair(vol, win_v, (2, 3))
 
+    def flip_own(i, carry):
+        transpose_plane(win_v, 2 + i, flipped_v, 1 + i)
+        return carry
+
+    lax.fori_loop(0, 2, flip_own, 0)
+
     @alone
     def _():
         convolve_own(win_v, 2, ahead1, own_pre)
@@ -309,54 +325,6 @@
 
     loads[2].wait()
     expand_weight(w2, ahead2, back2)
-
-    def on_side(side, act_low, act_high):
-        pl.when(jnp.logical_and(side == 0, has_low))(act_low)
-        pl.when(jnp.logical_and(side == 1, has_high))(act_high)
-
-    def side_of(i):
-        return lax.rem(1 - core + i, 2)
-
-    def volume_side(i, carry):
-        side = side_of(i)
-        on_side(side, lambda: to_high(1).wait_recv(), lambda: to_low(0).wait_recv())
-        slot = 1 + 3 * side
-        prepare(vol, slot, win_v, slot)
-
-        @alone
-        def _():
-            add_outer(win_v, slot, ahead1, own_pre, side)
-            at = pl.ds(pl.multiple_of(side * 256, 256), 256)
-            pre[at, :] += dot(planes_of(win_v, slot), ahead1[1])
-
-        hide(own_pre, side * 256, 1 + side, None)
-        prepare(hid, 1 + side, win_h, 1 + side)
-
-        @pl.when(i == 1)
-        def _():
-            convolve_own(win_h, 1, ahead2, acc)
-            add_outer(win_h, 3 * (1 - side), ahead2, acc, 1 - side)
-
-        on_side(side, lambda: to_high(0).wait_recv(), lambda: to_low(1).wait_recv())
-        prepare(vol, 5 * side, win_v, 5 * side)
-
-        @alone
-        def _():
-            add_outer(win_v, 5 * side, ahead1, pre, side)
-
-        inside = jnp.logical_or(jnp.logical_and(side == 0, has_low), jnp.logical_and(side == 1, has_high))
-        hide(pre, side * 256, 3 * side, inside)
-        prepare(hid, 3 * side, win_h, 3 * side)
-        return carry
-
-    lax.fori_loop(0, 2, volume_side, 0)
-
-    @alone
-    def _():
-        side = side_of(1)
-        add_outer(win_h, 3 * side, ahead2, acc, side)
-
-    loads[3].wait()
 
     def halo(buffer, which, side):
         if side == 0:
@@ -366,11 +334,6 @@
         return pltpu.make_async_remote_copy(
             buffer.at[2], buffer.at[0], g_send.at[2 * which + 1], g_recv.at[2 * which + 1], high, MESH
         )
-
-    def send_halo(buffer, which, side):
-        @pl.when(has_high if side else has_low)
-        def _():
-            halo(buffer, which, side).start()
 
     def second_stage(plane, carry):
         for j in range(QUADS):
@@ -382,11 +345,53 @@
             g2[plane + 1, :, cols] = (cot[plane, :, cols].astype(F32) * slope).astype(BF16)
         return carry
 
-    second_stage(0, 0)
-    send_halo(g2, 0, 0)
-    second_stage(1, 0)
-    send_halo(g2, 0, 1)
-
+    def send_side(buffer, which, side):
+        on_side(side, lambda: halo(buffer, which, 0).start(), lambda: halo(buffer, which, 1).start())
+
+    loads[3].wait()
+
+    def volume_side(i, carry):
+        side = side_of(i)
+        on_side(side, lambda: to_high(1).wait_recv(), lambda: to_low(0).wait_recv())
+        slot = 1 + 3 * side
+        prepare(vol, slot, win_v, slot)
+
+        @alone
+        def _():
+            add_outer(win_v, slot, ahead1, own_pre, side)
+            at = pl.ds(pl.multiple_of(side * 256, 256), 256)
+            pre[at, :] += dot(planes_of(win_v, slot), ahead1[1])
+
+        hide(own_pre, side * 256, 1 + side, None)
+        prepare(hid, 1 + side, win_h, 1 + side)
+
+        @pl.when(i == 1)
+        def _():
+            convolve_own(win_h, 1, ahead2, acc)
+            add_outer(win_h, 3 * on_chip, ahead2, acc, on_chip)
+            second_stage(on_chip, 0)
+            send_side(g2, 0, on_chip)
+
+        on_side(side, lambda: to_high(0).wait_recv(), lambda: to_low(1).wait_recv())
+        prepare(vol, 5 * side, win_v, 5 * side)
+
+        @alone
+        def _():
+            add_outer(win_v, 5 * side, ahead1, pre, side)
+
+        inside = jnp.logical_or(jnp.logical_and(side == 0, has_low), jnp.logical_and(side == 1, has_high))
+        hide(pre, side * 256, 3 * side, inside)
+        prepare(hid, 3 * side, win_h, 3 * side)
+        return carry
+
+    lax.fori_loop(0, 2, volume_side, 0)
+
+    @alone
+    def _():
+        add_outer(win_h, 3 * over_link, ahead2, acc, over_link)
+
+    second_stage(over_link, 0)
+    send_side(g2, 0, over_link)
     features_store = pltpu.make_async_copy(feat, feat_hbm.at[0], store_sem.at[0])
     features_store.start()
 
@@ -424,7 +429,7 @@
                         starts = [to * 216 + (2 * pair + i) * 27 + (27 * xx) // 4 for i in range(2)]
                         both = jnp.concatenate([flat[pl.ds(s, 8), :] for s in starts], axis=0)
                         near[which, to * 4 + xx, 16 * pair : 16 * pair + 16, :] = both.astype(BF16)
-                for rx in range(4):
+                for rx in (2, 1, 3, 0):
                     other = lax.rem(x + rx, 4)
                     copy = pltpu.make_async_remote_copy(
                         near.at[which, to * 4 + other],
@@ -439,6 +444,8 @@
                     else:
                         pl.when(away != 0)(copy.start)
 
+    far_order = sorted(range(1, 16), key=lambda r: -far_hops(r))
+
     def send_far(which):
         each(near_copy, "wait_recv", which)
         total = near[which, me_near].astype(F32)
@@ -446,14 +453,16 @@
             total = total + near_in[which, r].astype(F32)
         for zz in range(8):
             far[which, zz] = total[8 * zz : 8 * zz + 8]
-        each(far_copy, "start", which)
+        for r in far_order:
+            far_copy(which, r).start()
 
     lane = lax.broadcasted_iota(jnp.int32, (8, 128), 1)
     begin = (96 * x) % 128 + 432 * core
     skip_rows, skip_lanes = begin // 128, begin % 128
 
     def finish(which, out):
-        each(far_copy, "wait_recv", which)
+        for r in reversed(far_order):
+            far_copy(which, r).wait_recv()
         total = far[which, z]
         for r in range(1, 16):
             total = total + far_in[which, r]
@@ -473,7 +482,12 @@
 
     flip_planes(win_h, 0, flipped_h)
     kernel_gradient(flipped_h, win_g2, 1, product, flat, functools.partial(send_near, 1))
-    flip_planes(win_v, 1, flipped_v)
+
+    def flip_outer(i, carry):
+        transpose_plane(win_v, 1 + 3 * i, flipped_v, 3 * i)
+        return carry
+
+    lax.fori_loop(0, 2, flip_outer, 0)
 
     @alone
     def _():
@@ -505,8 +519,9 @@
             add_outer(win_g2, 3 * side, back2, acc, side, dot_transposed)
 
         first_stage(side, 0)
-        on_side(side, lambda: halo(g1, 1, 0).start(), lambda: halo(g1, 1, 1).start())
+        send_side(g1, 1, side)
         prepare(g1, 1 + side, win_g1, 1 + side)
+
         return carry
 
     lax.fori_loop(0, 2, g2_side, 0)

time: 39.5 us -> 39.1 us (0.990)
  Pallas kernels: 38.8 us -> 38.4 us
    pallas_call x1, Pallas kernels: 36.9 us -> 36.5 us  [per_device(): pl.pallas_call(functools.partial(kernel, slabs=slabs, scale=1.0 / math.sq...]
where the time goes in v4:
time: 39.1 us; the launch traced here: 39 us
  Pallas kernels  38.4 us (98%)
  between operations  0.64 us (2%)
    pallas_call x1, Pallas kernels, per_device(): pl.pallas_call(functools.partial(kernel, slabs=slabs, scale=1.0 / math.sq...  36.5 us
    pallas_call x1, Pallas kernels, per_device(): pl.pallas_call(hand_over, out_shape=(jax.ShapeDtypeStruct(volume.shape, B...  1.85 us

profile of v4, /device:TPU:1, one launch (start us, length us, event | category | flops | bytes accessed | tf_op | source)
XLA Modules:
  0.0 39.0 jit_solution(17213412921123668784)
XLA Ops:
  0.6 36.5 %shard_map.75 = (bf16[1,2,32,2048]{3,2,1,0:T(8,128)(2,1)}, bf16[1,2,32,2048]{3,2,1,0:T(8,128)(2,1)}, f32[8,128]{1,0:T(8,128)}, f32[8,128]{1,0:T(8,128)}) custom-call(bf16[1,2,32,2048]{3,2,1,0:T(8,128)(2,1)} %vol_hbm.1, bf16[1,2,32,2048]{3,2,1,0:T(8,128)(2,1)} %cot_hbm.1, bf16[3,3,3,64,64]{4,3,2,1,0:T(8,128)(2,1)} %w1_hbm.1, bf16[3,3,3,64,64]{4,3,2,1,0:T(8,128)(2,1)} %w2_hbm.1), custom_call_target="tpu_custom_call" | custom-call | tf_op jit(solution)/shard_map/pallas_call | solution.py:633
  37.1 1.8 %shard_map.76 = (bf16[1,2,32,2048]{3,2,1,0:T(8,128)(2,1)}, bf16[1,2,32,2048]{3,2,1,0:T(8,128)(2,1)}, f32[432]{0:T(512)}, f32[432]{0:T(512)}) custom-call(bf16[1,2,32,2048]{3,2,1,0:T(8,128)(2,1)} %get-tuple-element.8.feat_in, bf16[1,2,32,2048]{3,2,1,0:T(8,128)(2,1)} %get-tuple-element.9.back_in, f32[8,128]{1,0:T(8,128)} %get-tuple-element.10.first_in, ...), custom_call_target="tpu_custom_call" | custom-call | tf_op jit(solution)/shard_map/pallas_call | solution.py:648

commit v5 on v4

--- a/solution.py
+++ b/solution.py
@@ -350,6 +350,11 @@
 
     loads[3].wait()
 
+    def flip_side(side):
+        transpose_plane(win_v, 1 + 3 * side, flipped_v, 3 * side)
+        transpose_plane(win_h, 1 + side, flipped_h, 1 + side)
+        transpose_plane(win_h, 3 * side, flipped_h, 3 * side)
+
     def volume_side(i, carry):
         side = side_of(i)
         on_side(side, lambda: to_high(1).wait_recv(), lambda: to_low(0).wait_recv())
@@ -382,6 +387,11 @@
         inside = jnp.logical_or(jnp.logical_and(side == 0, has_low), jnp.logical_and(side == 1, has_high))
         hide(pre, side * 256, 3 * side, inside)
         prepare(hid, 3 * side, win_h, 3 * side)
+
+        @pl.when(i == 0)
+        def _():
+            flip_side(side)
+
         return carry
 
     lax.fori_loop(0, 2, volume_side, 0)
@@ -473,21 +483,8 @@
 
     prepare_pair(g2, win_g2, (1, 2))
 
-    def flip_planes(win, first, out):
-        def body(i, carry):
-            transpose_plane(win, first + i, out, i)
-            return carry
-
-        lax.fori_loop(0, 4, body, 0)
-
-    flip_planes(win_h, 0, flipped_h)
+    flip_side(over_link)
     kernel_gradient(flipped_h, win_g2, 1, product, flat, functools.partial(send_near, 1))
-
-    def flip_outer(i, carry):
-        transpose_plane(win_v, 1 + 3 * i, flipped_v, 3 * i)
-        return carry
-
-    lax.fori_loop(0, 2, flip_outer, 0)
 
     @alone
     def _():

time: 39.1 us -> 39 us (level)
  no operation moved by 1% of the time
where the time goes in v5:
time: 39 us; the launch traced here: 38.9 us
  Pallas kernels  38.3 us (98%)
  between operations  0.64 us (2%)
    pallas_call x1, Pallas kernels, per_device(): pl.pallas_call(functools.partial(kernel, slabs=slabs, scale=1.0 / math.sq...  36.4 us
    pallas_call x1, Pallas kernels, per_device(): pl.pallas_call(hand_over, out_shape=(jax.ShapeDtypeStruct(volume.shape, B...  1.85 us

profile of v5, /device:TPU:1, one launch (start us, length us, event | category | flops | bytes accessed | tf_op | source)
XLA Modules:
  0.0 38.9 jit_solution(9109914465108877774)
XLA Ops:
  0.6 36.4 %shard_map.75 = (bf16[1,2,32,2048]{3,2,1,0:T(8,128)(2,1)}, bf16[1,2,32,2048]{3,2,1,0:T(8,128)(2,1)}, f32[8,128]{1,0:T(8,128)}, f32[8,128]{1,0:T(8,128)}) custom-call(bf16[1,2,32,2048]{3,2,1,0:T(8,128)(2,1)} %vol_hbm.1, bf16[1,2,32,2048]{3,2,1,0:T(8,128)(2,1)} %cot_hbm.1, bf16[3,3,3,64,64]{4,3,2,1,0:T(8,128)(2,1)} %w1_hbm.1, bf16[3,3,3,64,64]{4,3,2,1,0:T(8,128)(2,1)} %w2_hbm.1), custom_call_target="tpu_custom_call" | custom-call | tf_op jit(solution)/shard_map/pallas_call | solution.py:630
  37.1 1.8 %shard_map.76 = (bf16[1,2,32,2048]{3,2,1,0:T(8,128)(2,1)}, bf16[1,2,32,2048]{3,2,1,0:T(8,128)(2,1)}, f32[432]{0:T(512)}, f32[432]{0:T(512)}) custom-call(bf16[1,2,32,2048]{3,2,1,0:T(8,128)(2,1)} %get-tuple-element.8.feat_in, bf16[1,2,32,2048]{3,2,1,0:T(8,128)(2,1)} %get-tuple-element.9.back_in, f32[8,128]{1,0:T(8,128)} %get-tuple-element.10.first_in, ...), custom_call_target="tpu_custom_call" | custom-call | tf_op jit(solution)/shard_map/pallas_call | solution.py:645
